TPU v7x, 512 devices: a whole 4x8x8 slice. The times are simulated.
512 devices in a mesh: dp: 32 (over x, z), fsdp: 16 (over y, core).
Axes of the slice: x: 4, y: 8, z: 8, core: 2. Of those that a mesh axis runs over, the one named last changes fastest.
Arguments:
- gradient: bfloat16 [32, 1024, 8192], P('dp', 'fsdp'), may hold values from -40 to 40
- error: bfloat16 [32, 1024, 8192], P('dp', 'fsdp'), may hold values from -6 to 6
- warm_start: bfloat16 [8192, 64], P('fsdp'), may hold values from -6 to 6
Outputs:
- update: bfloat16 [1024, 8192], P('fsdp')
- new_error: bfloat16 [32, 1024, 8192], P('dp', 'fsdp')
All inputs are finite; a program needn't handle non-finite values.
Results may differ from a plain program's by a relative error of at most 0.03.
Values may be sent and summed in bfloat16 or wider, within the bound.
A program may use at most 64 MiB of HBM per device.

v0:
```python
import jax
import jax.numpy as jnp
from jax import lax
from jax.sharding import PartitionSpec as P

ITERS = 2


def orthonormal(p_factor):
    gram_matrix = lax.psum(jnp.dot(p_factor.T, p_factor, precision=lax.Precision.HIGHEST), "fsdp")
    cholesky_factor = jnp.linalg.cholesky(gram_matrix)
    basis = jax.scipy.linalg.solve_triangular(cholesky_factor, p_factor.T, lower=True).T
    return basis.astype(jnp.bfloat16)


def on_device(gradient, error, warm_start):
    merged = (gradient[0].astype(jnp.float32) + error[0].astype(jnp.float32)).astype(jnp.bfloat16)
    replicas = lax.axis_size("dp")
    basis_b = None
    q_shard = warm_start
    for iteration in range(ITERS):
        p_factor = jnp.dot(
            merged,
            lax.all_gather(q_shard, "fsdp", axis=0, tiled=True),
            preferred_element_type=jnp.float32,
        )
        p_factor = lax.psum(p_factor, "dp")
        basis_b = orthonormal(p_factor)
        q_part = lax.psum_scatter(
            lax.dot_general(
                merged, basis_b, (((0,), (0,)), ((), ())), preferred_element_type=jnp.float32
            ),
            "fsdp",
            scatter_dimension=0,
            tiled=True,
        )
        q_part = lax.psum(q_part, "dp")
        q_shard = q_part.astype(jnp.bfloat16)
    mean_f32 = (
        lax.dot_general(
            basis_b,
            lax.all_gather(q_shard, "fsdp", axis=0, tiled=True),
            (((1,), (1,)), ((), ())),
            preferred_element_type=jnp.float32,
        )
        / replicas
    )
    update = mean_f32.astype(jnp.bfloat16)
    new_error = (merged.astype(jnp.float32) - mean_f32).astype(jnp.bfloat16)[None]
    return (update, new_error)


def solution(mesh):
    return jax.shard_map(
        on_device,
        mesh=mesh,
        in_specs=(P("dp", "fsdp", None), P("dp", "fsdp", None), P("fsdp", None)),
        out_specs=(P("fsdp", None), P("dp", "fsdp", None)),
        check_vma=False,
    )
```

profile of v0, /device:TPU:1, one launch (start us, length us, event | category | flops | bytes accessed | tf_op | source)
XLA Modules:
  0.0 937.5 jit_solution(4660571055524518554)
XLA Ops:
  7.2 0.7 all-gather.4.cloned.1.call-update
  7.9 1.8 fusion
  9.7 47.2 %all-gather.4.cloned.1.call-done = bf16[8192,64]{0,1:T(8,128)(2,1)} async-done(((bf16[512,64]{0,1:T(8,128)(2,1)}), bf16[8192,64]{0,1:T(8,128)(2,1)}) %all-gather.4.cloned.1.call-update) | async-done | bytes 1048592 | tf_op jit(solution)/shard_map/all_gather | solution.py:24
  56.9 1.6 fusion.12
  58.5 116.4 %psum.42 = f32[64,64]{1,0:T(8,128)S(1)} all-reduce(f32[64,64]{1,0:T(8,128)S(1)} %fusion.12), channel_id=1, replica_groups=mesh['dp'=32,'fsdp'=16] {'dp'}, use_global_device_ids=true, to_apply=%region_0.0 | all-reduce | flops 4096 | bytes 32768 | tf_op jit(solution)/shard_map/psum | solution.py:27
  175.2 69.8 %psum.43 = f32[64,64]{0,1:T(8,128)S(1)} all-reduce(f32[64,64]{0,1:T(8,128)S(1)} %fusion.13), channel_id=1, replica_groups=mesh['dp'=32,'fsdp'=16] {'fsdp'}, use_global_device_ids=true, to_apply=%region_1.0 | all-reduce | flops 4096 | bytes 32768 | tf_op jit(solution)/shard_map/psum | solution.py:10
  245.1 5.8 cholesky.44
  251.6 0.7 fusion.2
  252.3 4.9 custom-call.6
  257.5 1.8 fusion.16
  259.3 53.9 %reduce-scatter.3.cloned.1.call-done = f32[512,64]{0,1:T(8,128)} async-done(((f32[8192,64]{0,1:T(8,128)}), f32[512,64]{0,1:T(8,128)}) %reduce-scatter.3.cloned.1.call-update) | async-done | bytes 131088 | tf_op jit(solution)/shard_map/reduce_scatter | solution.py:29
  313.2 116.2 %all-reduce.2 = bf16[512,64]{0,1:T(8,128)(2,1)} all-reduce(f32[512,64]{0,1:T(8,128)} %reduce-scatter.3.cloned.1.call-done), channel_id=1, replica_groups=mesh['dp'=32,'fsdp'=16] {'dp'}, use_global_device_ids=true, to_apply=%region_5.0 | all-reduce | flops 32768 | bytes 196608 | tf_op jit(solution)/shard_map/psum | solution.py:37
  429.5 62.9 %all-gather.6.cloned.1.call-done = bf16[8192,64]{0,1:T(8,128)(2,1)} async-done(((bf16[512,64]{0,1:T(8,128)(2,1)}), bf16[8192,64]{0,1:T(8,128)(2,1)}) %all-gather.6.cloned.1.call-update) | async-done | bytes 1048592 | tf_op jit(solution)/shard_map/all_gather | solution.py:24
  492.4 1.6 fusion.14
  494.1 116.4 %psum.45 = f32[64,64]{1,0:T(8,128)S(1)} all-reduce(f32[64,64]{1,0:T(8,128)S(1)} %fusion.14), channel_id=1, replica_groups=mesh['dp'=32,'fsdp'=16] {'dp'}, use_global_device_ids=true, to_apply=%region_6.0 | all-reduce | flops 4096 | bytes 32768 | tf_op jit(solution)/shard_map/psum | solution.py:27
  610.7 69.8 %psum.46 = f32[64,64]{0,1:T(8,128)S(1)} all-reduce(f32[64,64]{0,1:T(8,128)S(1)} %fusion.15), channel_id=1, replica_groups=mesh['dp'=32,'fsdp'=16] {'fsdp'}, use_global_device_ids=true, to_apply=%region_7.0 | all-reduce | flops 4096 | bytes 32768 | tf_op jit(solution)/shard_map/psum | solution.py:10
  680.6 5.8 cholesky.55
  687.1 0.7 fusion.3
  687.8 4.9 custom-call.7
  693.0 1.8 fusion.17
  694.8 53.9 %reduce-scatter.5.cloned.1.call-done = f32[512,64]{0,1:T(8,128)} async-done(((f32[8192,64]{0,1:T(8,128)}), f32[512,64]{0,1:T(8,128)}) %reduce-scatter.5.cloned.1.call-update) | async-done | bytes 131088 | tf_op jit(solution)/shard_map/reduce_scatter | solution.py:29
  748.7 116.3 %all-reduce.3 = bf16[512,64]{0,1:T(8,128)(2,1)} all-reduce(f32[512,64]{0,1:T(8,128)} %reduce-scatter.5.cloned.1.call-done), channel_id=1, replica_groups=mesh['dp'=32,'fsdp'=16] {'dp'}, use_global_device_ids=true, to_apply=%region_9.12 | all-reduce | flops 32768 | bytes 196608 | tf_op jit(solution)/shard_map/psum | solution.py:37
  865.1 62.9 %all-gather.8.cloned.1.call-done = bf16[8192,64]{0,1:T(8,128)(2,1)} async-done(((bf16[512,64]{0,1:T(8,128)(2,1)}), bf16[8192,64]{0,1:T(8,128)(2,1)}) %all-gather.8.cloned.1.call-update) | async-done | bytes 1048592 | tf_op jit(solution)/shard_map/all_gather | solution.py:42
  927.9 3.0 fusion.1
  (21 shorter events, 2.7 us)
Async XLA Ops:
  7.2 49.7 %all-gather.4.cloned.1.call-start = ((), (), s32[]{:S(2)}) async-start(), calls=%async_computation.2 | async-start | bytes 1114112 | tf_op jit(solution)/shard_map/all_gather | solution.py:24
  7.9 305.3 %reduce-scatter.3.cloned.1.call-start = ((), (), s32[]{:S(2)}) async-start(), calls=%async_computation.3 | async-start | bytes 2228224 | tf_op jit(solution)/shard_map/reduce_scatter | solution.py:29
  259.3 233.2 %all-gather.6.cloned.1.call-start = ((), (), s32[]{:S(2)}) async-start(), calls=%async_computation.4 | async-start | bytes 1114112 | tf_op jit(solution)/shard_map/all_gather | solution.py:24
  429.5 319.2 %reduce-scatter.5.cloned.1.call-start = ((), (), s32[]{:S(2)}) async-start(), calls=%async_computation.5 | async-start | bytes 2228224 | tf_op jit(solution)/shard_map/reduce_scatter | solution.py:29
  694.7 233.2 %all-gather.8.cloned.1.call-start = ((), (), s32[]{:S(2)}) async-start(), calls=%async_computation.6 | async-start | bytes 1114112 | tf_op jit(solution)/shard_map/all_gather | solution.py:42
Sparse Core Ops, SparseCore 0:
  10.1 46.7 all-gather.3
  259.4 53.8 reduce-scatter.2
  429.6 62.7 all-gather.5
  694.9 53.7 reduce-scatter.4
  865.2 62.7 all-gather.7
where the time goes:
time: 938 us; the launch traced here: 937 us
  blocking collectives  605 us (64%)
  waiting for transfers between devices  282 us (30%)
  other arithmetic  25.9 us (3%)
  between operations  13.9 us (1%)
  matrix products  10.8 us (1%)
    psum x2, blocking collectives, on_device(): p_factor = lax.psum(p_factor, 'dp')  233 us
    psum x2, blocking collectives, on_device(): q_part = lax.psum(q_part, 'dp')  233 us
    all_gather x3, waiting for transfers between devices, on_device(): lax.all_gather(q_shard, 'fsdp', axis=0, tiled=True)  173 us
    psum x2, blocking collectives, orthonormal(): lax.psum(jnp.dot(p_factor.T, p_factor, precision=lax.Precision.HIGHEST),...  140 us
    reduce_scatter x2, waiting for transfers between devices, on_device(): lax.psum_scatter(lax.dot_general(merged, basis_b, (((0,), (0,)), ((), ())...  108 us
  transfers between devices with their start and end apart: 5, of which 5 were waited for; matrix products, arithmetic and copies ran while one was open for 0% of the time, Pallas kernels for 0%

commit v1 on v0

v1 whole, which is shorter than its diff:
```python
import functools

import jax
import jax.numpy as jnp
from jax import lax
from jax.experimental import pallas as pl
from jax.experimental.pallas import tpu as pltpu
from jax.sharding import PartitionSpec as P

MESH = pl.DeviceIdType.MESH
F32, BF16 = jnp.float32, jnp.bfloat16
NX, NY, NZ = 4, 8, 8
RANK = 64
HALF = RANK // 2


def dot(a, b, contract=((1,), (0,))):
    return lax.dot_general(a, b, (contract, ((), ())), precision=lax.Precision.HIGHEST, preferred_element_type=F32)


def by_distance(n):
    return sorted(range(1, n), key=lambda o: (-min(o, n - o), o))


def pack(a):
    return jnp.concatenate([a[:HALF], a[HALF:]], axis=1)


def unpack(a):
    return jnp.concatenate([a[:, :RANK], a[:, RANK:]], axis=0)


def inverse_factor(packed):
    lane = lax.broadcasted_iota(jnp.int32, (8, 2 * RANK), 1)
    sub = lax.broadcasted_iota(jnp.int32, (8, 2 * RANK), 0)
    rolled = pltpu.roll(packed, RANK, 1)
    rows = []
    for b in range(RANK // 8):
        source = packed if b < HALF // 8 else rolled
        r = (8 * b) % HALF
        rows.append(jnp.where(lane < RANK, source[r : r + 8], (lane - RANK == sub + 8 * b).astype(F32)))
    for k in range(RANK):
        b, r = divmod(k, 8)
        pivot_row = rows[b][r : r + 1, :]
        scaled = pivot_row * (1.0 / pivot_row[:, k : k + 1])
        for i in range(b, RANK // 8):
            column = rows[i][:, k : k + 1]
            new = rows[i] - column * scaled
            rows[i] = jnp.where(sub > r, new, rows[i]) if i == b else new
    out = []
    for b in range(RANK // 8):
        diag = jnp.sum(jnp.where(lane == sub + 8 * b, rows[b], 0.0), axis=1, keepdims=True)
        out.append(rows[b] * lax.rsqrt(diag))
    return jnp.concatenate(out, axis=0)[:, RANK:]


def kernel(
    g_ref, e_ref, w_ref, upd_ref, err_ref,
    gv, ev, merged, xland, zsend, zland, m, q0, px, pz, gsend, gcore, gy, usend, ucore, uy, ufull, qland, upd, err,
    in_sem, out_sem, q0_send, q0_recv, xs_send, xs_recv, zs_send, zs_recv,
    px_send, px_recv, pz_send, pz_recv, gc_send, gc_recv, gy_send, gy_recv, uc_send, uc_recv, uy_send, uy_recv,
    uf_send, uf_recv, qz_send, qz_recv, qx_send, qx_recv, qc_send, qc_recv,
):
    nd, rows, cb = merged.shape
    wide = NZ * cb
    d, f = lax.axis_index("dp"), lax.axis_index("fsdp")
    x, z, y, k = d // NZ, d % NZ, f // 2, f % 2

    def at_x(o):
        return {"dp": ((x + o) % NX) * NZ + z, "fsdp": f}

    def at_z(o):
        return {"dp": x * NZ + (z + o) % NZ, "fsdp": f}

    def at_y(o):
        return {"dp": d, "fsdp": ((y + o) % NY) * 2 + k}

    partner = {"dp": d, "fsdp": y * 2 + 1 - k}

    def send(src, dst, ssem, rsem, to):
        copy = pltpu.make_async_remote_copy(
            src_ref=src, dst_ref=dst, send_sem=ssem, recv_sem=rsem, device_id=to, device_id_type=MESH
        )
        copy.start()
        return copy

    sent = []

    loads = []
    for i in range(NX):
        cols = pl.ds(i * wide, wide)
        for j, (src, dst) in enumerate(((g_ref, gv), (e_ref, ev))):
            copy = pltpu.make_async_copy(src.at[0, :, cols], dst.at[:, cols], in_sem.at[j, i])
            copy.start()
            loads.append(copy)

    barrier = pltpu.get_barrier_semaphore()
    greeted = [at_x(o) for o in range(1, NX)] + [at_z(o) for o in range(1, NZ)]
    greeted += [{"dp": d, "fsdp": (f + o) % (2 * NY)} for o in range(1, 2 * NY)]
    for to in greeted:
        pl.semaphore_signal(barrier, inc=1, device_id=to, device_id_type=MESH)

    per = w_ref.shape[0] // cb
    source = d // per
    part = d % per

    @pl.when(f == source)
    def _():
        q0[...] = w_ref[pl.ds(pl.multiple_of(part * cb, cb), cb), :].astype(F32).T.astype(BF16)

    for copy in loads:
        copy.wait()

    def merge(i, _):
        cols = pl.ds(pl.multiple_of(i * cb, cb), cb)
        merged[i] = (gv[:, cols].astype(F32) + ev[:, cols].astype(F32)).astype(BF16)
        return 0

    lax.fori_loop(0, nd, merge, 0)
    pl.semaphore_wait(barrier, len(greeted))

    zorder = by_distance(NZ) + [0]
    xcopies = []
    for i, o in enumerate(zorder):
        w = (z + o) % NZ
        xcopies.append([
            send(merged.at[((x + xo) % NX) * NZ + w], xland.at[xo - 1, i], xs_send.at[xo - 1, i], xs_recv.at[xo - 1, i], at_x(xo))
            for xo in by_distance(NX)
        ])
        sent += xcopies[-1]

    others = 2 * NY - 1

    def q0_copy(o):
        return pltpu.make_async_remote_copy(
            src_ref=q0, dst_ref=q0, send_sem=q0_send.at[o], recv_sem=q0_recv,
            device_id={"dp": d, "fsdp": (f + o + 1) % (2 * NY)}, device_id_type=MESH,
        )

    @pl.when(f == source)
    def _():
        for o in range(others):
            q0_copy(o).start()

    zcopies = []
    for i, o in enumerate(zorder):
        for copy in xcopies[i]:
            copy.wait_recv()
        total = merged[x * NZ + (z + o) % NZ].astype(F32)
        for j in range(NX - 1):
            total = total + xland[j, i].astype(F32)
        if o:
            zsend[i] = total.astype(BF16)
            zcopies.append(send(zsend.at[i], zland.at[i], zs_send.at[i], zs_recv.at[i], at_z(o)))
    for i, copy in enumerate(zcopies):
        copy.wait_recv()
        total = total + zland[i].astype(F32)
    sent += zcopies
    m[...] = total

    @pl.when(f != source)
    def _():
        q0_copy(0).wait_recv()

    @pl.when(f == source)
    def _():
        for o in range(others):
            q0_copy(o).wait_send()

    def sum_dp(value, use, beside=None):
        px[use, x] = pack(value)
        copies = [
            send(px.at[use, x], px.at[use, x], px_send.at[use, o - 1], px_recv.at[use, o - 1], at_x(o)) for o in by_distance(NX)
        ]
        for copy in copies:
            copy.wait_recv()
        total = px[use, 0]
        for i in range(1, NX):
            total = total + px[use, i]
        sent.extend(copies)
        pz[use, z] = total
        copies = [
            send(pz.at[use, z], pz.at[use, z], pz_send.at[use, o - 1], pz_recv.at[use, o - 1], at_z(o)) for o in by_distance(NZ)
        ]
        extra = beside() if beside is not None else None
        for copy in copies:
            copy.wait_recv()
        total = pz[use, 0]
        for i in range(1, NZ):
            total = total + pz[use, i]
        sent.extend(copies)
        return unpack(total), extra

    def sum_y(buf, use, ssem, rsem):
        copies = [send(buf.at[use, y], buf.at[use, y], ssem.at[use, o - 1], rsem.at[use, o - 1], at_y(o)) for o in by_distance(NY)]
        sent.extend(copies)

        def finish():
            for copy in copies:
                copy.wait_recv()
            total = buf[use, 0]
            for i in range(1, NY):
                total = total + buf[use, i]
            return total

        return finish

    def over_rows(p_t, use):
        gsend[use] = pack(dot(p_t, p_t, ((1,), (1,))))
        gram_copy = send(gsend.at[use], gcore.at[use], gc_send.at[use], gc_recv.at[use], partner)
        u_t = dot(p_t, m[...])
        half = cb // 2
        usend[use, 0] = u_t[:, :half]
        usend[use, 1] = u_t[:, half:]
        u_copy = send(usend.at[use, 1 - k], ucore.at[use], uc_send.at[use], uc_recv.at[use], partner)
        sent.extend([gram_copy, u_copy])
        gram_copy.wait_recv()
        gy[use, y] = gsend[use] + gcore[use]
        gram = sum_y(gy, use, gy_send, gy_recv)
        u_copy.wait_recv()
        uy[use, y] = usend[use, k] + ucore[use]
        u_half = sum_y(uy, use, uy_send, uy_recv)
        return gram, u_half

    p_t, _ = sum_dp(dot(q0[...].astype(F32), m[...], ((1,), (1,))), 0)
    gram, u_half = over_rows(p_t, 0)
    gram = gram()
    lane = lax.broadcasted_iota(jnp.int32, (HALF, 2 * RANK), 1)
    sub = lax.broadcasted_iota(jnp.int32, (HALF, 2 * RANK), 0)
    on_diag = (lane == sub) | (lane == sub + HALF + RANK)
    trace = jnp.sum(jnp.sum(jnp.where(on_diag, gram, 0.0), axis=1, keepdims=True), axis=0, keepdims=True)
    scale = lax.rsqrt(trace)
    ufull[k] = u_half() * scale
    u_copy = send(ufull.at[k], ufull.at[k], uf_send, uf_recv, partner)
    u_copy.wait_recv()
    sent.append(u_copy)
    u_t = jnp.concatenate([ufull[0], ufull[1]], axis=1)

    p_t, inverse = sum_dp(dot(u_t, m[...], ((1,), (1,))), 1, lambda: inverse_factor(gram * scale * scale))
    p_t = dot(inverse, p_t)
    gram, u_half = over_rows(p_t, 1)
    inverse = inverse_factor(gram())
    basis_b = dot(inverse, p_t).T.astype(BF16)
    qland[k, d] = dot(inverse, u_half()).astype(BF16)

    def q_z(o):
        return send(qland.at[k, d], qland.at[k, d], qz_send.at[o - 1], qz_recv.at[o - 1], at_z(o))

    def q_x(o, block):
        return [
            send(qland.at[k, block], qland.at[k, block], qx_send.at[xo - 1, o], qx_recv.at[xo - 1, o], at_x(xo))
            for xo in by_distance(NX)
        ]

    def q_core(slot, block):
        sent.append(send(qland.at[k, block], qland.at[k, block], qc_send.at[slot], qc_recv.at[slot], partner))

    zcopies = {o: q_z(o) for o in by_distance(NZ)}
    sent += zcopies.values()
    near = [0] + by_distance(NZ)[::-1]
    xcopies = {}
    for o in near:
        if o:
            zcopies[o].wait_recv()
        block = x * NZ + (z - o) % NZ
        xcopies[o] = q_x(o, block)
        sent += xcopies[o]
        q_core(o, block)
    for o in near:
        for copy, xo in zip(xcopies[o], by_distance(NX)):
            copy.wait_recv()
            q_core(xo * NZ + o, ((x - xo) % NX) * NZ + (z - o) % NZ)

    outs = []
    for xo in range(NX):
        xs = (x - xo) % NX

        def finish(o, _):
            block = xs * NZ + (z - o) % NZ
            pltpu.make_async_remote_copy(
                src_ref=qland.at[k, block], dst_ref=qland.at[1 - k, block],
                send_sem=qc_send.at[xo * NZ + o], recv_sem=qc_recv.at[xo * NZ + o],
                device_id=partner, device_id_type=MESH,
            ).wait_recv()
            q_t = jnp.concatenate([qland[0, block], qland[1, block]], axis=1)
            mean = jnp.dot(basis_b, q_t, preferred_element_type=F32) * (1.0 / nd)
            cols = pl.ds(pl.multiple_of(block * cb, cb), cb)
            upd[:, cols] = mean.astype(BF16)
            err[:, cols] = (merged[block].astype(F32) - mean).astype(BF16)
            return 0

        lax.fori_loop(0, NZ, finish, 0)
        cols = pl.ds(pl.multiple_of(xs * wide, wide), wide)
        for j, (src, dst) in enumerate(((upd, upd_ref), (err, err_ref.at[0]))):
            copy = pltpu.make_async_copy(src.at[:, cols], dst.at[:, cols], out_sem.at[j, xo])
            copy.start()
            outs.append(copy)
    for copy in sent:
        copy.wait_send()
    for copy in outs:
        copy.wait()


def on_device(gradient, error, warm_start):
    nd = NX * NZ
    _, rows, width = gradient.shape
    cb = width // nd
    dma = pltpu.SemaphoreType.DMA
    anywhere = pl.BlockSpec(memory_space=pl.ANY)
    return pl.pallas_call(
        kernel,
        out_shape=(
            jax.ShapeDtypeStruct((rows, width), BF16),
            jax.ShapeDtypeStruct((1, rows, width), BF16),
        ),
        in_specs=[anywhere, anywhere, pl.BlockSpec(memory_space=pltpu.VMEM)],
        out_specs=(anywhere, anywhere),
        scratch_shapes=[
            pltpu.VMEM((rows, width), BF16),
            pltpu.VMEM((rows, width), BF16),
            pltpu.VMEM((nd, rows, cb), BF16),
            pltpu.VMEM((NX - 1, NZ, rows, cb), BF16),
            pltpu.VMEM((NZ - 1, rows, cb), BF16),
            pltpu.VMEM((NZ - 1, rows, cb), BF16),
            pltpu.VMEM((rows, cb), F32),
            pltpu.VMEM((RANK, cb), BF16),
            pltpu.VMEM((2, NX, HALF, 2 * RANK), F32),
            pltpu.VMEM((2, NZ, HALF, 2 * RANK), F32),
            pltpu.VMEM((2, HALF, 2 * RANK), F32),
            pltpu.VMEM((2, HALF, 2 * RANK), F32),
            pltpu.VMEM((2, NY, HALF, 2 * RANK), F32),
            pltpu.VMEM((2, 2, RANK, cb // 2), F32),
            pltpu.VMEM((2, RANK, cb // 2), F32),
            pltpu.VMEM((2, NY, RANK, cb // 2), F32),
            pltpu.VMEM((2, RANK, cb // 2), F32),
            pltpu.VMEM((2, nd, RANK, cb // 2), BF16),
            pltpu.VMEM((rows, width), BF16),
            pltpu.VMEM((rows, width), BF16),
            dma((2, NX)), dma((2, NX)), dma((2 * NY - 1,)), dma,
            dma((NX - 1, NZ)), dma((NX - 1, NZ)), dma((NZ - 1,)), dma((NZ - 1,)),
            dma((2, NX - 1)), dma((2, NX - 1)), dma((2, NZ - 1)), dma((2, NZ - 1)),
            dma((2,)), dma((2,)), dma((2, NY - 1)), dma((2, NY - 1)),
            dma((2,)), dma((2,)), dma((2, NY - 1)), dma((2, NY - 1)),
            dma, dma, dma((NZ - 1,)), dma((NZ - 1,)), dma((NX - 1, NZ)), dma((NX - 1, NZ)), dma((nd,)), dma((nd,)),
        ],
        compiler_params=pltpu.CompilerParams(collective_id=0, has_side_effects=True, vmem_limit_bytes=32 << 20),
        cost_estimate=pl.CostEstimate(flops=4 * rows * width * RANK, bytes_accessed=8 * rows * width, transcendentals=0),
    )(gradient, error, warm_start)


def solution(mesh):
    return jax.shard_map(
        on_device,
        mesh=mesh,
        in_specs=(P("dp", "fsdp", None), P("dp", "fsdp", None), P("fsdp", None)),
        out_specs=(P("fsdp", None), P("dp", "fsdp", None)),
        check_vma=False,
    )
```

time: 938 us -> 107 us (0.11)
  blocking collectives: 605 us -> 0 us
  waiting for transfers between devices: 282 us -> 0 us
  Pallas kernels: 0 us -> 100 us
  other arithmetic: 25.9 us -> 0 us
  between operations: 13.9 us -> 0.65 us
  matrix products: 10.8 us -> 0 us
    psum x6 -> x0, blocking collectives: 605 us -> none  [the longest x2 233 us: on_device(): p_factor = lax.psum(p_factor, 'dp')]
    all_gather x3 -> x0, waiting for transfers between devices: 173 us -> none  [on_device(): lax.all_gather(q_shard, 'fsdp', axis=0, tiled=True)]
    reduce_scatter x2 -> x0, waiting for transfers between devices: 108 us -> none  [on_device(): lax.psum_scatter(lax.dot_general(merged, basis_b, (((0,), (0,)), ((), ())...]
    pallas_call x0 -> x1, Pallas kernels: none -> 100 us  [on_device(): pl.pallas_call(kernel, out_shape=(jax.ShapeDtypeStruct((rows, width), BF1...]
    another operation x10 -> x0, other arithmetic: 24.1 us -> none  [the longest x6 13 us: orthonormal(): cholesky_factor = jnp.linalg.cholesky(gram_matrix)]
    dot_general x7 -> x0, matrix products: 10.3 us -> none  [the longest x2 3.54 us: on_device(): lax.dot_general(merged, basis_b, (((0,), (0,)), ((), ())), preferred_elem...]
  transfers between devices with their start and end apart: 5 -> 0, of which waited for: 5 -> 0; matrix products, arithmetic and copies ran while one was open for 0% -> 0% of each run, Pallas kernels for 0% -> 0%
where the time goes in v1:
time: 107 us; the launch traced here: 106 us
  Pallas kernels  100 us (93%)
  local copies, waits for them, and re-layouts  5.34 us (5%)
    pallas_call x1, Pallas kernels, on_device(): pl.pallas_call(kernel, out_shape=(jax.ShapeDtypeStruct((rows, width), BF1...  100 us
    unnamed x7, local copies, waits for them, and re-layouts  5.34 us

profile of v1, /device:TPU:1, one launch (start us, length us, event | category | flops | bytes accessed | tf_op | source)
XLA Modules:
  0.0 106.3 jit_solution(14700075013672868265)
XLA Ops:
  0.6 1.0 copy.5.w_ref
  1.6 0.0 copy-start
  1.6 1.2 %copy-done = bf16[1,64,8192]{2,1,0:T(8,128)(2,1)S(1)} copy-done((bf16[1,64,8192]{2,1,0:T(8,128)(2,1)S(1)}, bf16[1,64,8192]{2,1,0:T(8,128)(2,1)}, u32[]{:S(2)}) %copy-start) | copy-done | bytes 1048600
  2.8 0.0 copy-start.1
  2.8 1.2 %copy-done.1 = bf16[1,64,8192]{2,1,0:T(8,128)(2,1)S(1)} copy-done((bf16[1,64,8192]{2,1,0:T(8,128)(2,1)S(1)}, bf16[1,64,8192]{2,1,0:T(8,128)(2,1)}, u32[]{:S(2)}) %copy-start.1) | copy-done | bytes 1048600
  4.0 100.3 %shard_map.50 = (bf16[64,8192]{1,0:T(8,128)(2,1)S(1)}, bf16[1,64,8192]{2,1,0:T(8,128)(2,1)S(1)}) custom-call(bf16[1,64,8192]{2,1,0:T(8,128)(2,1)S(1)} %copy-done, bf16[1,64,8192]{2,1,0:T(8,128)(2,1)S(1)} %copy-done.1, bf16[512,64]{1,0:T(8,128)(2,1)S(1)} %copy.5.w_ref), custom_call_target="tpu_custom_call" | custom-call | flops 134217728 | bytes 4194304 | tf_op jit(solution)/shard_map/pallas_call | solution.py:310
  104.4 1.0 copy.8
  105.3 1.0 copy.9
Async XLA Ops:
  1.6 1.2 %copy-start = (bf16[1,64,8192]{2,1,0:T(8,128)(2,1)S(1)}, bf16[1,64,8192]{2,1,0:T(8,128)(2,1)}, u32[]{:S(2)}) copy-start(bf16[1,64,8192]{2,1,0:T(8,128)(2,1)} %g_ref.1) | copy-start | bytes 3145732
  2.8 1.2 %copy-start.1 = (bf16[1,64,8192]{2,1,0:T(8,128)(2,1)S(1)}, bf16[1,64,8192]{2,1,0:T(8,128)(2,1)}, u32[]{:S(2)}) copy-start(bf16[1,64,8192]{2,1,0:T(8,128)(2,1)} %e_ref.1) | copy-start | bytes 3145732

commit v2 on v0

v2 whole, which is shorter than its diff:
```python
import functools

import jax
import jax.numpy as jnp
from jax import lax
from jax.experimental import pallas as pl
from jax.experimental.pallas import tpu as pltpu
from jax.sharding import PartitionSpec as P

MESH = pl.DeviceIdType.MESH
F32, BF16 = jnp.float32, jnp.bfloat16
NX, NY, NZ = 4, 8, 8
RANK = 64
HALF = RANK // 2
TAIL = 16
GROUPS = 4


def split(a):
    high = a.astype(BF16)
    rest = a - high.astype(F32)
    middle = rest.astype(BF16)
    return jnp.concatenate([high, middle, (rest - middle.astype(F32)).astype(BF16)], axis=0)


def exact(a, b, contract=((1,), (0,))):
    terms = lax.dot_general(a, b, (contract, ((), ())), preferred_element_type=F32)
    return terms[:RANK] + (terms[RANK : 2 * RANK] + terms[2 * RANK :])


def dot(a, b):
    return jnp.dot(a, b, precision=lax.Precision.HIGHEST, preferred_element_type=F32)


def by_distance(n):
    return sorted(range(1, n), key=lambda o: (-min(o, n - o), o))


def pack(a):
    return jnp.concatenate([a[:HALF], a[HALF:]], axis=1)


def unpack(a):
    return jnp.concatenate([a[:, :RANK], a[:, RANK:]], axis=0)


def inverse_factor(packed):
    lane = lax.broadcasted_iota(jnp.int32, (8, 2 * RANK), 1)
    sub = lax.broadcasted_iota(jnp.int32, (8, 2 * RANK), 0)
    rolled = pltpu.roll(packed, RANK, 1)
    full, n = (8, 2 * RANK), RANK // 8
    a = []
    for b in range(n):
        source = packed if b < n // 2 else rolled
        r = (8 * b) % HALF
        a.append(jnp.where(lane < RANK, source[r : r + 8], (lane - RANK == sub + 8 * b).astype(F32)))
    for b in range(n):
        row = [jnp.broadcast_to(a[b][j : j + 1, :], full) for j in range(8)]
        diag = {(i, j): jnp.broadcast_to(row[i][:, 8 * b + j : 8 * b + j + 1], full) for i in range(8) for j in range(i, 8)}
        column = {(j, v): jnp.broadcast_to(a[v][:, 8 * b + j : 8 * b + j + 1], full) for j in range(8) for v in range(b + 1, n)}
        scaled = []
        for j in range(8):
            inverse = 1.0 / diag[j, j]
            for i in range(j + 1, 8):
                factor = diag[j, i] * inverse
                for c in range(i, 8):
                    diag[i, c] = diag[i, c] - factor * diag[j, c]
                row[i] = row[i] - factor * row[j]
                for v in range(b + 1, n):
                    column[i, v] = column[i, v] - factor * column[j, v]
            scaled.append(row[j] * inverse)
        for v in range(b + 1, n):
            for j in range(8):
                a[v] = a[v] - column[j, v] * scaled[j]
        for j in range(1, 8):
            a[b] = jnp.where(sub == j, row[j], a[b])
    out = []
    for b in range(n):
        pivot = jnp.sum(jnp.where(lane == sub + 8 * b, a[b], 0.0), axis=1, keepdims=True)
        out.append(a[b] * lax.rsqrt(pivot))
    return jnp.concatenate(out, axis=0)[:, RANK:]


def kernel(
    g_ref, e_ref, w_ref, qland, merged, basis,
    gv, ev, tails, xland, zsend, zland, tland, tsum, town, tx, mc, q0, px, pz, pf,
    in_sem, w_sem, q0_send, q0_recv, x_send, x_recv, z_send, z_recv, t_send, t_recv, tx_send, tx_recv,
    my_send, my_recv, mk_send, mk_recv, px_send, px_recv, pz_send, pz_recv, py_send, py_recv, pk_send, pk_recv,
    qz_send, qz_recv, qx_send, qx_recv, qk_send, qk_recv,
):
    nd, rows, cb = merged.shape
    body = rows - TAIL
    half = cb // 2
    d, f = lax.axis_index("dp"), lax.axis_index("fsdp")
    x, z, y, k = d // NZ, d % NZ, f // 2, f % 2

    def at_x(o):
        return {"dp": ((x + o) % NX) * NZ + z, "fsdp": f}

    def at_z(o):
        return {"dp": x * NZ + (z + o) % NZ, "fsdp": f}

    def at_y(o):
        return {"dp": d, "fsdp": ((y + o) % NY) * 2 + k}

    partner = {"dp": d, "fsdp": f + 1 - 2 * k}

    def remote(src, dst, ssem, rsem, to):
        return pltpu.make_async_remote_copy(
            src_ref=src, dst_ref=dst, send_sem=ssem, recv_sem=rsem, device_id=to, device_id_type=MESH
        )

    def send(src, dst, ssem, rsem, to):
        remote(src, dst, ssem, rsem, to).start()

    def arrived(as_much, sem):
        remote(as_much, as_much, sem, sem, partner).wait_recv()

    def left(as_much, sem):
        remote(as_much, as_much, sem, sem, partner).wait_send()

    loads = [pltpu.make_async_copy(g_ref.at[0], gv, in_sem.at[0]), pltpu.make_async_copy(e_ref.at[0], ev, in_sem.at[1])]
    for copy in loads:
        copy.start()

    barrier = pltpu.get_barrier_semaphore()
    greeted = [at_z(o) for o in by_distance(NZ)] + [at_y(o) for o in by_distance(NY)] + [at_x(o) for o in by_distance(NX)]
    greeted.append(partner)
    for to in greeted:
        pl.semaphore_signal(barrier, inc=1, device_id=to, device_id_type=MESH)

    per = w_ref.shape[1] // cb
    source = d // per
    w_copy = pltpu.make_async_copy(w_ref.at[:, pl.ds(pl.multiple_of((d % per) * cb, cb), cb)], q0, w_sem)
    is_source = f == source
    is_relay = (k == source % 2) & (y != source // 2)

    @pl.when(is_source)
    def _():
        w_copy.start()

    for copy in loads:
        copy.wait()

    zorder = by_distance(NZ) + [0]
    for i, o in enumerate(zorder):
        w = (z + o) % NZ
        for t in range(NX):
            block = t * NZ + w
            cols = pl.ds(pl.multiple_of(block * cb, cb), cb)
            value = (gv[:, cols].astype(F32) + ev[:, cols].astype(F32)).astype(BF16)
            merged[block] = value
            tails[i, t * TAIL : (t + 1) * TAIL] = value[body:]
    pl.semaphore_wait(barrier, len(greeted))

    def mine(i, xo):
        return ((x + xo) % NX) * NZ + (z + zorder[i]) % NZ

    for i, o in enumerate(zorder):
        if o:
            send(tails.at[i], tland.at[i], t_send, t_recv, at_z(o))
        for j, xo in enumerate(by_distance(NX)):
            send(merged.at[mine(i, xo), pl.ds(0, body)], xland.at[i, j], x_send, x_recv.at[i], at_x(xo))

    @pl.when(is_source)
    def _():
        w_copy.wait()
        send(q0, q0, q0_send, q0_recv, partner)
        for o in by_distance(NY):
            send(q0, q0, q0_send, q0_recv, at_y(o))

    def finish_tails():
        arrived(tland, t_recv)
        total = tails[NZ - 1].astype(F32)
        for i in range(NZ - 1):
            total = total + tland[i].astype(F32)
        town[...] = total
        tsum[...] = total.astype(BF16)
        for j, xo in enumerate(by_distance(NX)):
            rows_of = pl.ds(pl.multiple_of(((x + xo) % NX) * TAIL, TAIL), TAIL)
            send(tsum.at[rows_of], tx.at[j], tx_send, tx_recv, at_x(xo))

    for i, o in enumerate(zorder):
        if i == 6:
            finish_tails()

            @pl.when(is_relay)
            def _():
                arrived(q0, q0_recv)
                send(q0, q0, q0_send, q0_recv, partner)

        arrived(xland.at[i], x_recv.at[i])
        total = merged[mine(i, 0)][:body].astype(F32)
        for j in range(NX - 1):
            total = total + xland[i, j].astype(F32)
        if o:
            zsend[i] = total.astype(BF16)
            send(zsend.at[i], zland.at[i], z_send, z_recv, at_z(o))
    arrived(tx, tx_recv)
    tail = town[pl.ds(pl.multiple_of(x * TAIL, TAIL), TAIL), :]
    for j in range(NX - 1):
        tail = tail + tx[j].astype(F32)
    arrived(zland, z_recv)
    for i in range(NZ - 1):
        total = total + zland[i].astype(F32)
    m = jnp.concatenate([total, tail], axis=0).astype(BF16)

    @pl.when(~(is_source | is_relay))
    def _():
        arrived(q0, q0_recv)

    mc[k, y] = m
    for o in by_distance(NY):
        send(mc.at[k, y], mc.at[k, y], my_send, my_recv, at_y(o))

    def sum_dp(value, use, beside=None):
        px[use, x] = pack(value)
        for o in by_distance(NX):
            send(px.at[use, x], px.at[use, x], px_send, px_recv.at[use], at_x(o))
        arrived(px.at[use, pl.ds(0, NX - 1)], px_recv.at[use])
        total = (px[use, 0] + px[use, 1]) + (px[use, 2] + px[use, 3])
        pz[use, z] = total
        for o in by_distance(NZ):
            send(pz.at[use, z], pz.at[use, z], pz_send, pz_recv.at[use], at_z(o))
        extra = beside() if beside is not None else None
        arrived(pz.at[use, pl.ds(0, NZ - 1)], pz_recv.at[use])
        total = pz[use, 0]
        for i in range(1, NZ):
            total = total + pz[use, i]
        return total, extra

    lane = lax.broadcasted_iota(jnp.int32, (HALF, 2 * RANK), 1)
    sub = lax.broadcasted_iota(jnp.int32, (HALF, 2 * RANK), 0)

    def over_rows(packed, use):
        pf[use, k, y] = packed
        for o in by_distance(NY):
            send(pf.at[use, k, y], pf.at[use, k, y], py_send, py_recv.at[use], at_y(o))
        if use == 0:
            arrived(mc.at[k, pl.ds(0, NY - 1)], my_recv)
            send(mc.at[k], mc.at[k], mk_send, mk_recv, partner)
        arrived(pf.at[use, k, pl.ds(0, NY - 1)], py_recv.at[use])
        send(pf.at[use, k], pf.at[use, k], pk_send, pk_recv.at[use], partner)
        if use == 0:
            arrived(mc.at[1 - k], mk_recv)
        arrived(pf.at[use, 1 - k], pk_recv.at[use])
        u_t, gram = 0.0, 0.0
        for c in range(2):
            for i in range(0, NY, 4):
                parts = []
                for j in range(i, i + 4, 2):
                    one, two = pf[use, c, j], pf[use, c, j + 1]
                    upper = jnp.where(lane < RANK, one, pltpu.roll(two, RANK, 1))
                    lower = jnp.where(lane < RANK, pltpu.roll(one, RANK, 1), two)
                    parts.append(jnp.concatenate([upper, lower], axis=0))
                p = split(jnp.concatenate(parts, axis=1))
                u_t = u_t + exact(p, mc[c, i : i + 4].reshape(4 * rows, cb))
                gram = gram + exact(p, p, ((1,), (1,)))
        gram = gram[:, :RANK] + (gram[:, RANK : 2 * RANK] + gram[:, 2 * RANK :])
        return u_t, pack(gram)

    p, _ = sum_dp(
        lax.dot_general(q0[...], m, (((1,), (1,)), ((), ())), preferred_element_type=F32), 0
    )
    u_t, gram = over_rows(p, 0)
    on_diag = (lane == sub) | (lane == sub + HALF + RANK)
    trace = jnp.sum(jnp.sum(jnp.where(on_diag, gram, 0.0), axis=1, keepdims=True), axis=0, keepdims=True)
    scale = lax.rsqrt(trace)

    p, inverse = sum_dp(
        exact(split(u_t * scale), mc[k, y], ((1,), (1,))), 1, lambda: inverse_factor(gram * scale * scale)
    )
    p_t = dot(inverse, unpack(p))
    u_t, gram = over_rows(pack(p_t), 1)
    inverse = inverse_factor(gram)
    q_t = dot(inverse, u_t).astype(BF16)
    qland[0, d] = q_t[:, :half]
    qland[1, d] = q_t[:, half:]

    for o in by_distance(NZ):
        send(qland.at[k, d], qland.at[k, d], qz_send, qz_recv.at[o - 1], at_z(o))
    basis[...] = dot(inverse, p_t).T.astype(BF16)
    near = [0] + by_distance(NZ)[::-1]
    for o in near:
        block = x * NZ + (z - o) % NZ
        if o:
            arrived(qland.at[k, block], qz_recv.at[o - 1])
        for xo in by_distance(NX):
            send(qland.at[k, block], qland.at[k, block], qx_send, qx_recv.at[o], at_x(xo))
        if o:
            send(qland.at[k, block], qland.at[k, block], qk_send, qk_recv, partner)
    for o in near:
        arrived(qland.at[k, pl.ds(0, NX - 1)], qx_recv.at[o])
        for xo in by_distance(NX):
            block = ((x - xo) % NX) * NZ + (z - o) % NZ
            send(qland.at[k, block], qland.at[k, block], qk_send, qk_recv, partner)
    arrived(qland.at[1 - k, pl.ds(0, nd - 1)], qk_recv)

    left(xland, x_send)
    left(tland, t_send)
    left(tx, tx_send)
    left(zland, z_send)
    left(mc.at[k, pl.ds(0, NY - 1)], my_send)
    left(mc.at[k], mk_send)
    left(px.at[:, pl.ds(0, NX - 1)], px_send)
    left(pz.at[:, pl.ds(0, NZ - 1)], pz_send)
    left(pf.at[:, k, pl.ds(0, NY - 1)], py_send)
    left(pf.at[:, k], pk_send)
    left(qland.at[k, pl.ds(0, NZ - 1)], qz_send)
    left(qland.at[k, pl.ds(0, (NX - 1) * NZ)], qx_send)
    left(qland.at[k, pl.ds(0, nd - 1)], qk_send)

    @pl.when(is_source)
    def _():
        left(mc.at[k], q0_send)

    @pl.when(is_relay)
    def _():
        left(q0, q0_send)


def decompress(q_ref, merged, basis, upd_ref, err_ref, upd, err, sem):
    nd, rows, cb = merged.shape
    per = nd // GROUPS
    wide = per * cb
    left = basis[...]
    copies = []
    for i in range(GROUPS):
        for j in range(per):
            block = i * per + j
            q_t = jnp.concatenate([q_ref[0, block], q_ref[1, block]], axis=1)
            mean = jnp.dot(left, q_t, preferred_element_type=F32) * (1.0 / nd)
            cols = pl.ds(block * cb, cb)
            upd[:, cols] = mean.astype(BF16)
            err[:, cols] = (merged[block].astype(F32) - mean).astype(BF16)
        cols = pl.ds(i * wide, wide)
        for j, (src, dst) in enumerate(((upd, upd_ref), (err, err_ref.at[0]))):
            copy = pltpu.make_async_copy(src.at[:, cols], dst.at[:, cols], sem.at[j, i])
            copy.start()
            copies.append(copy)
    for copy in copies:
        copy.wait()


def on_device(gradient, error, warm_start):
    nd = NX * NZ
    _, rows, width = gradient.shape
    cb = width // nd
    dma = pltpu.SemaphoreType.DMA
    hbm = pl.BlockSpec(memory_space=pltpu.HBM)
    vmem = pl.BlockSpec(memory_space=pltpu.VMEM)
    small = (HALF, 2 * RANK)
    q, merged, basis = pl.pallas_call(
        kernel,
        out_shape=(
            pltpu.VMEM((2, nd, RANK, cb // 2), BF16),
            pltpu.VMEM((nd, rows, cb), BF16),
            pltpu.VMEM((rows, RANK), BF16),
        ),
        in_specs=[hbm, hbm, hbm],
        out_specs=(vmem, vmem, vmem),
        scratch_shapes=[
            pltpu.VMEM((rows, width), BF16),
            pltpu.VMEM((rows, width), BF16),
            pltpu.VMEM((NZ, NX * TAIL, cb), BF16),
            pltpu.VMEM((NZ, NX - 1, rows - TAIL, cb), BF16),
            pltpu.VMEM((NZ - 1, rows - TAIL, cb), BF16),
            pltpu.VMEM((NZ - 1, rows - TAIL, cb), BF16),
            pltpu.VMEM((NZ - 1, NX * TAIL, cb), BF16),
            pltpu.VMEM((NX * TAIL, cb), BF16),
            pltpu.VMEM((NX * TAIL, cb), F32),
            pltpu.VMEM((NX - 1, TAIL, cb), BF16),
            pltpu.VMEM((2, NY, rows, cb), BF16),
            pltpu.VMEM((RANK, cb), BF16),
            pltpu.VMEM((2, NX) + small, F32),
            pltpu.VMEM((2, NZ) + small, F32),
            pltpu.VMEM((2, 2, NY) + small, F32),
            dma((2,)), dma, dma, dma, dma, dma((NZ,)), dma, dma, dma, dma, dma, dma,
            dma, dma, dma, dma, dma, dma((2,)), dma, dma((2,)), dma, dma((2,)), dma, dma((2,)),
            dma, dma((NZ - 1,)), dma, dma((NZ,)), dma, dma,
        ],
        compiler_params=pltpu.CompilerParams(collective_id=0, has_side_effects=True, vmem_limit_bytes=32 << 20),
        cost_estimate=pl.CostEstimate(flops=4 * rows * width * RANK, bytes_accessed=8 * rows * width, transcendentals=0),
    )(*(pltpu.with_memory_space_constraint(v, pltpu.HBM) for v in (gradient, error, warm_start.T)))
    q, merged, basis = (pltpu.with_memory_space_constraint(v, pltpu.VMEM) for v in (q, merged, basis))
    return pl.pallas_call(
        decompress,
        out_shape=(jax.ShapeDtypeStruct((rows, width), BF16), jax.ShapeDtypeStruct((1, rows, width), BF16)),
        in_specs=[vmem, vmem, vmem],
        out_specs=(hbm, hbm),
        scratch_shapes=[pltpu.VMEM((rows, width), BF16), pltpu.VMEM((rows, width), BF16), dma((2, GROUPS))],
        compiler_params=pltpu.CompilerParams(vmem_limit_bytes=16 << 20),
        cost_estimate=pl.CostEstimate(flops=2 * rows * width * RANK, bytes_accessed=8 * rows * width, transcendentals=0),
    )(q, merged, basis)


def solution(mesh):
    return jax.shard_map(
        on_device,
        mesh=mesh,
        in_specs=(P("dp", "fsdp", None), P("dp", "fsdp", None), P("fsdp", None)),
        out_specs=(P("fsdp", None), P("dp", "fsdp", None)),
        check_vma=False,
    )
```

time: 938 us -> 79.4 us (0.08)
  blocking collectives: 605 us -> 0 us
  waiting for transfers between devices: 282 us -> 0 us
  Pallas kernels: 0 us -> 78.6 us
  other arithmetic: 25.9 us -> 0 us
  between operations: 13.9 us -> 0.64 us
  matrix products: 10.8 us -> 0 us
    psum x6 -> x0, blocking collectives: 605 us -> none  [the longest x2 233 us: on_device(): p_factor = lax.psum(p_factor, 'dp')]
    all_gather x3 -> x0, waiting for transfers between devices: 173 us -> none  [on_device(): lax.all_gather(q_shard, 'fsdp', axis=0, tiled=True)]
    reduce_scatter x2 -> x0, waiting for transfers between devices: 108 us -> none  [on_device(): lax.psum_scatter(lax.dot_general(merged, basis_b, (((0,), (0,)), ((), ())...]
    pallas_call x0 -> x2, Pallas kernels: none -> 78.6 us  [the longest x1 77.1 us: on_device(): pl.pallas_call(kernel, out_shape=(pltpu.VMEM((2, nd, RANK, cb // 2), BF16...]
    another operation x10 -> x0, other arithmetic: 24.1 us -> none  [the longest x6 13 us: orthonormal(): cholesky_factor = jnp.linalg.cholesky(gram_matrix)]
    dot_general x7 -> x0, matrix products: 10.3 us -> none  [the longest x2 3.54 us: on_device(): lax.dot_general(merged, basis_b, (((0,), (0,)), ((), ())), preferred_elem...]
  transfers between devices with their start and end apart: 5 -> 0, of which waited for: 5 -> 0; matrix products, arithmetic and copies ran while one was open for 0% -> 0% of each run, Pallas kernels for 0% -> 0%
where the time goes in v2:
time: 79.4 us; the launch traced here: 79.3 us
  Pallas kernels  78.6 us (99%)
    pallas_call x1, Pallas kernels, on_device(): pl.pallas_call(kernel, out_shape=(pltpu.VMEM((2, nd, RANK, cb // 2), BF16...  77.1 us

profile of v2, /device:TPU:1, one launch (start us, length us, event | category | flops | bytes accessed | tf_op | source)
XLA Modules:
  0.0 79.3 jit_solution(15310103271372057502)
XLA Ops:
  0.6 77.1 %shard_map.50 = (bf16[2,32,64,128]{3,2,1,0:T(8,128)(2,1)S(1)}, bf16[32,64,256]{2,1,0:T(8,128)(2,1)S(1)}, bf16[64,64]{1,0:T(8,128)(2,1)S(1)}) custom-call(bf16[1,64,8192]{2,1,0:T(8,128)(2,1)} %g_ref.1, bf16[1,64,8192]{2,1,0:T(8,128)(2,1)} %e_ref.1, bf16[64,512]{1,0:T(8,128)(2,1)} %bitcast.1), custom_call_target="tpu_custom_call" | custom-call | flops 134217728 | bytes 4194304 | tf_op jit(solution)/shard_map/pallas_call | solution.py:353
  77.7 1.6 %shard_map.51 = (bf16[64,8192]{1,0:T(8,128)(2,1)}, bf16[1,64,8192]{2,1,0:T(8,128)(2,1)}) custom-call(bf16[2,32,64,128]{3,2,1,0:T(8,128)(2,1)S(1)} %get-tuple-element.5.q_ref, bf16[32,64,256]{2,1,0:T(8,128)(2,1)S(1)} %get-tuple-element.6.merged, bf16[64,64]{1,0:T(8,128)(2,1)S(1)} %get-tuple-element.7.basis), custom_call_target="tpu_custom_call" | custom-call | flops 67108864 | bytes 4194304 | tf_op jit(solution)/shard_map/pallas_call | solution.py:386

commit v3 on v2

--- a/solution.py
+++ b/solution.py
@@ -12,7 +12,7 @@
 NX, NY, NZ = 4, 8, 8
 RANK = 64
 HALF = RANK // 2
-TAIL = 16
+TAIL = 32
 GROUPS = 4
 
 
@@ -83,10 +83,10 @@
 
 def kernel(
     g_ref, e_ref, w_ref, qland, merged, basis,
-    gv, ev, tails, xland, zsend, zland, tland, tsum, town, tx, mc, q0, px, pz, pf,
+    gv, ev, xland, zsend, zland, tland, tsum, tx, mc, q0, px, pz, pf,
     in_sem, w_sem, q0_send, q0_recv, x_send, x_recv, z_send, z_recv, t_send, t_recv, tx_send, tx_recv,
     my_send, my_recv, mk_send, mk_recv, px_send, px_recv, pz_send, pz_recv, py_send, py_recv, pk_send, pk_recv,
-    qz_send, qz_recv, qx_send, qx_recv, qk_send, qk_recv,
+    qz_send, qz_recv, qx_send, qx_recv, qu_send, qu_recv, qv_send, qv_recv, qw_recv, qk_send, qk_recv,
 ):
     nd, rows, cb = merged.shape
     body = rows - TAIL
@@ -148,19 +148,19 @@
         for t in range(NX):
             block = t * NZ + w
             cols = pl.ds(pl.multiple_of(block * cb, cb), cb)
-            value = (gv[:, cols].astype(F32) + ev[:, cols].astype(F32)).astype(BF16)
-            merged[block] = value
-            tails[i, t * TAIL : (t + 1) * TAIL] = value[body:]
+            merged[block] = (gv[:, cols].astype(F32) + ev[:, cols].astype(F32)).astype(BF16)
     pl.semaphore_wait(barrier, len(greeted))
 
     def mine(i, xo):
         return ((x + xo) % NX) * NZ + (z + zorder[i]) % NZ
 
+    opposite = NX // 2
     for i, o in enumerate(zorder):
         if o:
-            send(tails.at[i], tland.at[i], t_send, t_recv, at_z(o))
-        for j, xo in enumerate(by_distance(NX)):
-            send(merged.at[mine(i, xo), pl.ds(0, body)], xland.at[i, j], x_send, x_recv.at[i], at_x(xo))
+            send(merged.at[mine(i, opposite), pl.ds(body, TAIL)], tland.at[i], t_send, t_recv, at_z(o))
+        send(merged.at[mine(i, opposite), pl.ds(0, body)], xland.at[i, pl.ds(2 * rows, body)], x_send, x_recv.at[i], at_x(opposite))
+        for j in range(2):
+            send(merged.at[mine(i, 1 - 2 * j)], xland.at[i, pl.ds(j * rows, rows)], x_send, x_recv.at[i], at_x(1 - 2 * j))
 
     @pl.when(is_source)
     def _():
@@ -171,14 +171,11 @@
 
     def finish_tails():
         arrived(tland, t_recv)
-        total = tails[NZ - 1].astype(F32)
+        total = merged[mine(NZ - 1, opposite)][body:].astype(F32)
         for i in range(NZ - 1):
             total = total + tland[i].astype(F32)
-        town[...] = total
         tsum[...] = total.astype(BF16)
-        for j, xo in enumerate(by_distance(NX)):
-            rows_of = pl.ds(pl.multiple_of(((x + xo) % NX) * TAIL, TAIL), TAIL)
-            send(tsum.at[rows_of], tx.at[j], tx_send, tx_recv, at_x(xo))
+        send(tsum, tx, tx_send, tx_recv, at_x(opposite))
 
     for i, o in enumerate(zorder):
         if i == 6:
@@ -190,20 +187,17 @@
                 send(q0, q0, q0_send, q0_recv, partner)
 
         arrived(xland.at[i], x_recv.at[i])
-        total = merged[mine(i, 0)][:body].astype(F32)
-        for j in range(NX - 1):
-            total = total + xland[i, j].astype(F32)
+        landed = xland[i].astype(F32)
+        total = merged[mine(i, 0)].astype(F32) + (landed[:rows] + landed[rows : 2 * rows])
+        total = jnp.concatenate([total[:body] + landed[2 * rows :], total[body:]], axis=0)
         if o:
             zsend[i] = total.astype(BF16)
             send(zsend.at[i], zland.at[i], z_send, z_recv, at_z(o))
-    arrived(tx, tx_recv)
-    tail = town[pl.ds(pl.multiple_of(x * TAIL, TAIL), TAIL), :]
-    for j in range(NX - 1):
-        tail = tail + tx[j].astype(F32)
     arrived(zland, z_recv)
     for i in range(NZ - 1):
         total = total + zland[i].astype(F32)
-    m = jnp.concatenate([total, tail], axis=0).astype(BF16)
+    arrived(tx, tx_recv)
+    m = jnp.concatenate([total[:body], total[body:] + tx[...].astype(F32)], axis=0).astype(BF16)
 
     @pl.when(~(is_source | is_relay))
     def _():
@@ -230,7 +224,6 @@
         return total, extra
 
     lane = lax.broadcasted_iota(jnp.int32, (HALF, 2 * RANK), 1)
-    sub = lax.broadcasted_iota(jnp.int32, (HALF, 2 * RANK), 0)
 
     def over_rows(packed, use):
         pf[use, k, y] = packed
@@ -241,11 +234,9 @@
             send(mc.at[k], mc.at[k], mk_send, mk_recv, partner)
         arrived(pf.at[use, k, pl.ds(0, NY - 1)], py_recv.at[use])
         send(pf.at[use, k], pf.at[use, k], pk_send, pk_recv.at[use], partner)
-        if use == 0:
-            arrived(mc.at[1 - k], mk_recv)
-        arrived(pf.at[use, 1 - k], pk_recv.at[use])
-        u_t, gram = 0.0, 0.0
-        for c in range(2):
+
+        def factors(c):
+            terms = []
             for i in range(0, NY, 4):
                 parts = []
                 for j in range(i, i + 4, 2):
@@ -253,48 +244,88 @@
                     upper = jnp.where(lane < RANK, one, pltpu.roll(two, RANK, 1))
                     lower = jnp.where(lane < RANK, pltpu.roll(one, RANK, 1), two)
                     parts.append(jnp.concatenate([upper, lower], axis=0))
-                p = split(jnp.concatenate(parts, axis=1))
-                u_t = u_t + exact(p, mc[c, i : i + 4].reshape(4 * rows, cb))
-                gram = gram + exact(p, p, ((1,), (1,)))
-        gram = gram[:, :RANK] + (gram[:, RANK : 2 * RANK] + gram[:, 2 * RANK :])
-        return u_t, pack(gram)
+                terms.append(split(jnp.concatenate(parts, axis=1)))
+            return terms
+
+        def right(c, terms):
+            return sum(exact(p, mc[c, 4 * i : 4 * i + 4].reshape(4 * rows, cb)) for i, p in enumerate(terms))
+
+        def square(terms):
+            return sum(exact(p, p, ((1,), (1,))) for p in terms)
+
+        def squares(c):
+            total = pf[use, c, 0] * pf[use, c, 0]
+            for i in range(1, NY):
+                total = total + pf[use, c, i] * pf[use, c, i]
+            return total
+
+        def finish(gram):
+            return pack(gram[:, :RANK] + (gram[:, RANK : 2 * RANK] + gram[:, 2 * RANK :]))
+
+        terms = factors(k)
+        u_t = right(k, terms)
+        if use == 0:
+            norm = squares(k)
+            arrived(mc.at[1 - k], mk_recv)
+        else:
+            gram = square(terms)
+        arrived(pf.at[use, 1 - k], pk_recv.at[use])
+        terms = factors(1 - k)
+        u_t = u_t + right(1 - k, terms)
+        if use == 0:
+            norm = norm + squares(1 - k)
+            norm = jnp.sum(jnp.sum(norm, axis=1, keepdims=True), axis=0, keepdims=True)
+            return u_t, norm, lambda: finish(square(factors(0)) + square(factors(1)))
+        return u_t, finish(gram + square(terms))
 
     p, _ = sum_dp(
         lax.dot_general(q0[...], m, (((1,), (1,)), ((), ())), preferred_element_type=F32), 0
     )
-    u_t, gram = over_rows(p, 0)
-    on_diag = (lane == sub) | (lane == sub + HALF + RANK)
-    trace = jnp.sum(jnp.sum(jnp.where(on_diag, gram, 0.0), axis=1, keepdims=True), axis=0, keepdims=True)
-    scale = lax.rsqrt(trace)
+    u_t, norm, gram = over_rows(p, 0)
+    scale = lax.rsqrt(norm)
 
     p, inverse = sum_dp(
-        exact(split(u_t * scale), mc[k, y], ((1,), (1,))), 1, lambda: inverse_factor(gram * scale * scale)
+        exact(split(u_t * scale), mc[k, y], ((1,), (1,))), 1, lambda: inverse_factor(gram() * scale * scale)
     )
     p_t = dot(inverse, unpack(p))
     u_t, gram = over_rows(pack(p_t), 1)
     inverse = inverse_factor(gram)
-    q_t = dot(inverse, u_t).astype(BF16)
-    qland[0, d] = q_t[:, :half]
-    qland[1, d] = q_t[:, half:]
+    q_t = dot(inverse, u_t)
+    qland[k, d] = jnp.where(k == 0, q_t[:, :half], q_t[:, half:]).astype(BF16)
 
     for o in by_distance(NZ):
         send(qland.at[k, d], qland.at[k, d], qz_send, qz_recv.at[o - 1], at_z(o))
+    first, last = pl.ds(0, HALF), pl.ds(HALF, HALF)
+
+    def to_x(block, at):
+        send(qland.at[k, block, first], qland.at[k, block, first], qu_send, qu_recv, at_x(opposite))
+        for j in range(2):
+            send(qland.at[k, block], qland.at[k, block], qx_send, qx_recv.at[at], at_x(1 - 2 * j))
+
+    send(qland.at[k, d, last], qland.at[k, d, last], qv_send, qv_recv, at_x(opposite))
+    to_x(d, 0)
+    send(qland.at[k, d], qland.at[k, d], qk_send, qk_recv, partner)
     basis[...] = dot(inverse, p_t).T.astype(BF16)
-    near = [0] + by_distance(NZ)[::-1]
-    for o in near:
+    facing = ((x + opposite) % NX) * NZ
+    near = by_distance(NZ)[::-1]
+    for i, o in enumerate(near):
         block = x * NZ + (z - o) % NZ
-        if o:
-            arrived(qland.at[k, block], qz_recv.at[o - 1])
-        for xo in by_distance(NX):
-            send(qland.at[k, block], qland.at[k, block], qx_send, qx_recv.at[o], at_x(xo))
-        if o:
+        arrived(qland.at[k, block], qz_recv.at[o - 1])
+        to_x(block, o)
+        send(qland.at[k, block], qland.at[k, block], qk_send, qk_recv, partner)
+        if i == 1:
+            arrived(qland.at[k, facing + z, last], qv_recv)
+            for zo in by_distance(NZ):
+                send(qland.at[k, facing + z, last], qland.at[k, facing + z, last], qv_send, qw_recv, at_z(zo))
+    for o in [0] + near:
+        arrived(qland.at[k, pl.ds(0, 2)], qx_recv.at[o])
+        for j in range(2):
+            block = ((x + 1 - 2 * j) % NX) * NZ + (z - o) % NZ
             send(qland.at[k, block], qland.at[k, block], qk_send, qk_recv, partner)
-    for o in near:
-        arrived(qland.at[k, pl.ds(0, NX - 1)], qx_recv.at[o])
-        for xo in by_distance(NX):
-            block = ((x - xo) % NX) * NZ + (z - o) % NZ
-            send(qland.at[k, block], qland.at[k, block], qk_send, qk_recv, partner)
-    arrived(qland.at[1 - k, pl.ds(0, nd - 1)], qk_recv)
+    arrived(qland.at[k, pl.ds(0, NZ - 1), last], qw_recv)
+    arrived(qland.at[k, pl.ds(0, NZ), first], qu_recv)
+    send(qland.at[k, pl.ds(facing, NZ)], qland.at[k, pl.ds(facing, NZ)], qk_send, qk_recv, partner)
+    arrived(qland.at[1 - k], qk_recv)
 
     left(xland, x_send)
     left(tland, t_send)
@@ -307,8 +338,10 @@
     left(pf.at[:, k, pl.ds(0, NY - 1)], py_send)
     left(pf.at[:, k], pk_send)
     left(qland.at[k, pl.ds(0, NZ - 1)], qz_send)
-    left(qland.at[k, pl.ds(0, (NX - 1) * NZ)], qx_send)
-    left(qland.at[k, pl.ds(0, nd - 1)], qk_send)
+    left(qland.at[k, pl.ds(0, 2 * NZ)], qx_send)
+    left(qland.at[k, pl.ds(0, NZ), first], qu_send)
+    left(qland.at[k, pl.ds(0, NZ), last], qv_send)
+    left(qland.at[k], qk_send)
 
     @pl.when(is_source)
     def _():
@@ -362,14 +395,12 @@
         scratch_shapes=[
             pltpu.VMEM((rows, width), BF16),
             pltpu.VMEM((rows, width), BF16),
-            pltpu.VMEM((NZ, NX * TAIL, cb), BF16),
-            pltpu.VMEM((NZ, NX - 1, rows - TAIL, cb), BF16),
-            pltpu.VMEM((NZ - 1, rows - TAIL, cb), BF16),
-            pltpu.VMEM((NZ - 1, rows - TAIL, cb), BF16),
-            pltpu.VMEM((NZ - 1, NX * TAIL, cb), BF16),
-            pltpu.VMEM((NX * TAIL, cb), BF16),
-            pltpu.VMEM((NX * TAIL, cb), F32),
-            pltpu.VMEM((NX - 1, TAIL, cb), BF16),
+            pltpu.VMEM((NZ, 3 * rows - TAIL, cb), BF16),
+            pltpu.VMEM((NZ - 1, rows, cb), BF16),
+            pltpu.VMEM((NZ - 1, rows, cb), BF16),
+            pltpu.VMEM((NZ - 1, TAIL, cb), BF16),
+            pltpu.VMEM((TAIL, cb), BF16),
+            pltpu.VMEM((TAIL, cb), BF16),
             pltpu.VMEM((2, NY, rows, cb), BF16),
             pltpu.VMEM((RANK, cb), BF16),
             pltpu.VMEM((2, NX) + small, F32),
@@ -377,7 +408,7 @@
             pltpu.VMEM((2, 2, NY) + small, F32),
             dma((2,)), dma, dma, dma, dma, dma((NZ,)), dma, dma, dma, dma, dma, dma,
             dma, dma, dma, dma, dma, dma((2,)), dma, dma((2,)), dma, dma((2,)), dma, dma((2,)),
-            dma, dma((NZ - 1,)), dma, dma((NZ,)), dma, dma,
+            dma, dma((NZ - 1,)), dma, dma((NZ,)), dma, dma, dma, dma, dma, dma, dma,
         ],
         compiler_params=pltpu.CompilerParams(collective_id=0, has_side_effects=True, vmem_limit_bytes=32 << 20),
         cost_estimate=pl.CostEstimate(flops=4 * rows * width * RANK, bytes_accessed=8 * rows * width, transcendentals=0),

time: 79.4 us -> 77.3 us (0.974)
  Pallas kernels: 78.6 us -> 76.5 us
    pallas_call x1, Pallas kernels: 77.1 us -> 74.9 us  [on_device(): pl.pallas_call(kernel, out_shape=(pltpu.VMEM((2, nd, RANK, cb // 2), BF16...]
where the time goes in v3:
time: 77.3 us; the launch traced here: 77.1 us
  Pallas kernels  76.5 us (99%)
    pallas_call x1, Pallas kernels, on_device(): pl.pallas_call(kernel, out_shape=(pltpu.VMEM((2, nd, RANK, cb // 2), BF16...  74.9 us
    pallas_call x1, Pallas kernels, on_device(): pl.pallas_call(decompress, out_shape=(jax.ShapeDtypeStruct((rows, width),...  1.59 us

profile of v3, /device:TPU:1, one launch (start us, length us, event | category | flops | bytes accessed | tf_op | source)
XLA Modules:
  0.0 77.1 jit_solution(12653671581493172860)
XLA Ops:
  0.6 74.9 %shard_map.50 = (bf16[2,32,64,128]{3,2,1,0:T(8,128)(2,1)S(1)}, bf16[32,64,256]{2,1,0:T(8,128)(2,1)S(1)}, bf16[64,64]{1,0:T(8,128)(2,1)S(1)}) custom-call(bf16[1,64,8192]{2,1,0:T(8,128)(2,1)} %g_ref.1, bf16[1,64,8192]{2,1,0:T(8,128)(2,1)} %e_ref.1, bf16[64,512]{1,0:T(8,128)(2,1)} %bitcast.1), custom_call_target="tpu_custom_call" | custom-call | flops 134217728 | bytes 4194304 | tf_op jit(solution)/shard_map/pallas_call | solution.py:386
  75.5 1.6 %shard_map.51 = (bf16[64,8192]{1,0:T(8,128)(2,1)}, bf16[1,64,8192]{2,1,0:T(8,128)(2,1)}) custom-call(bf16[2,32,64,128]{3,2,1,0:T(8,128)(2,1)S(1)} %get-tuple-element.5.q_ref, bf16[32,64,256]{2,1,0:T(8,128)(2,1)S(1)} %get-tuple-element.6.merged, bf16[64,64]{1,0:T(8,128)(2,1)S(1)} %get-tuple-element.7.basis), custom_call_target="tpu_custom_call" | custom-call | flops 67108864 | bytes 4194304 | tf_op jit(solution)/shard_map/pallas_call | solution.py:417

commit v4 on v3

--- a/solution.py
+++ b/solution.py
@@ -83,9 +83,10 @@
 
 def kernel(
     g_ref, e_ref, w_ref, qland, merged, basis,
-    gv, ev, xland, zsend, zland, tland, tsum, tx, mc, q0, px, pz, pf,
+    gv, ev, xland, zsend, zland, tland, tsum, tx, mc, q0, px, pz, pf, gx, ux, nx,
     in_sem, w_sem, q0_send, q0_recv, x_send, x_recv, z_send, z_recv, t_send, t_recv, tx_send, tx_recv,
-    my_send, my_recv, mk_send, mk_recv, px_send, px_recv, pz_send, pz_recv, py_send, py_recv, pk_send, pk_recv,
+    my_send, my_recv, px_send, px_recv, pz_send, pz_recv, py_send, py_recv, gx_send, gx_recv, ux_send, ux_recv,
+    nx_send, nx_recv,
     qz_send, qz_recv, qx_send, qx_recv, qu_send, qu_recv, qv_send, qv_recv, qw_recv, qk_send, qk_recv,
 ):
     nd, rows, cb = merged.shape
@@ -155,12 +156,23 @@
         return ((x + xo) % NX) * NZ + (z + zorder[i]) % NZ
 
     opposite = NX // 2
-    for i, o in enumerate(zorder):
-        if o:
-            send(merged.at[mine(i, opposite), pl.ds(body, TAIL)], tland.at[i], t_send, t_recv, at_z(o))
-        send(merged.at[mine(i, opposite), pl.ds(0, body)], xland.at[i, pl.ds(2 * rows, body)], x_send, x_recv.at[i], at_x(opposite))
+    pairs = [2, 1, 3, 0]
+
+    def first_of(i):
+        return 2 * ((z // 2 + pairs[i]) % (NZ // 2))
+
+    def two(i, xo):
+        return pl.ds(((x + xo) % NX) * NZ + first_of(i), 2)
+
+    for i in range(NZ // 2):
+        to = at_x(opposite)
+        send(merged.at[two(i, opposite), pl.ds(0, body)], xland.at[i, :, pl.ds(2 * rows, body)], x_send, x_recv.at[i], to)
         for j in range(2):
-            send(merged.at[mine(i, 1 - 2 * j)], xland.at[i, pl.ds(j * rows, rows)], x_send, x_recv.at[i], at_x(1 - 2 * j))
+            xo = 1 - 2 * j
+            send(merged.at[two(i, xo)], xland.at[i, :, pl.ds(j * rows, rows)], x_send, x_recv.at[i], at_x(xo))
+        for h in (2 * i, 2 * i + 1):
+            if h < NZ - 1:
+                send(merged.at[mine(h, opposite), pl.ds(body, TAIL)], tland.at[h], t_send, t_recv, at_z(zorder[h]))
 
     @pl.when(is_source)
     def _():
@@ -177,8 +189,13 @@
         tsum[...] = total.astype(BF16)
         send(tsum, tx, tx_send, tx_recv, at_x(opposite))
 
-    for i, o in enumerate(zorder):
-        if i == 6:
+    def block_sum(i, b):
+        landed = xland[i, b].astype(F32)
+        total = merged[x * NZ + first_of(i) + b].astype(F32) + (landed[:rows] + landed[rows : 2 * rows])
+        return jnp.concatenate([total[:body] + landed[2 * rows :], total[body:]], axis=0)
+
+    for i in range(NZ // 2):
+        if i == NZ // 2 - 1:
             finish_tails()
 
             @pl.when(is_relay)
@@ -187,15 +204,15 @@
                 send(q0, q0, q0_send, q0_recv, partner)
 
         arrived(xland.at[i], x_recv.at[i])
-        landed = xland[i].astype(F32)
-        total = merged[mine(i, 0)].astype(F32) + (landed[:rows] + landed[rows : 2 * rows])
-        total = jnp.concatenate([total[:body] + landed[2 * rows :], total[body:]], axis=0)
-        if o:
-            zsend[i] = total.astype(BF16)
-            send(zsend.at[i], zland.at[i], z_send, z_recv, at_z(o))
-    arrived(zland, z_recv)
-    for i in range(NZ - 1):
-        total = total + zland[i].astype(F32)
+        for b in range(2) if i < NZ // 2 - 1 else (1 - z % 2,):
+            at = 2 * i if i == NZ // 2 - 1 else 2 * i + b
+            zsend[at] = block_sum(i, b).astype(BF16)
+            to = {"dp": x * NZ + first_of(i) + b, "fsdp": f}
+            send(zsend.at[at], zland.at[z], z_send, z_recv, to)
+    total = block_sum(NZ // 2 - 1, z % 2)
+    arrived(zland.at[pl.ds(0, NZ - 1)], z_recv)
+    for o in range(1, NZ):
+        total = total + zland[(z + o) % NZ].astype(F32)
     arrived(tx, tx_recv)
     m = jnp.concatenate([total[:body], total[body:] + tx[...].astype(F32)], axis=0).astype(BF16)
 
@@ -203,9 +220,9 @@
     def _():
         arrived(q0, q0_recv)
 
-    mc[k, y] = m
+    mc[y] = m
     for o in by_distance(NY):
-        send(mc.at[k, y], mc.at[k, y], my_send, my_recv, at_y(o))
+        send(mc.at[y], mc.at[y], my_send, my_recv, at_y(o))
 
     def sum_dp(value, use, beside=None):
         px[use, x] = pack(value)
@@ -226,74 +243,68 @@
     lane = lax.broadcasted_iota(jnp.int32, (HALF, 2 * RANK), 1)
 
     def over_rows(packed, use):
-        pf[use, k, y] = packed
+        pf[use, y] = packed
         for o in by_distance(NY):
-            send(pf.at[use, k, y], pf.at[use, k, y], py_send, py_recv.at[use], at_y(o))
+            send(pf.at[use, y], pf.at[use, y], py_send, py_recv.at[use], at_y(o))
         if use == 0:
-            arrived(mc.at[k, pl.ds(0, NY - 1)], my_recv)
-            send(mc.at[k], mc.at[k], mk_send, mk_recv, partner)
-        arrived(pf.at[use, k, pl.ds(0, NY - 1)], py_recv.at[use])
-        send(pf.at[use, k], pf.at[use, k], pk_send, pk_recv.at[use], partner)
-
-        def factors(c):
-            terms = []
-            for i in range(0, NY, 4):
-                parts = []
-                for j in range(i, i + 4, 2):
-                    one, two = pf[use, c, j], pf[use, c, j + 1]
-                    upper = jnp.where(lane < RANK, one, pltpu.roll(two, RANK, 1))
-                    lower = jnp.where(lane < RANK, pltpu.roll(one, RANK, 1), two)
-                    parts.append(jnp.concatenate([upper, lower], axis=0))
-                terms.append(split(jnp.concatenate(parts, axis=1)))
-            return terms
-
-        def right(c, terms):
-            return sum(exact(p, mc[c, 4 * i : 4 * i + 4].reshape(4 * rows, cb)) for i, p in enumerate(terms))
-
-        def square(terms):
-            return sum(exact(p, p, ((1,), (1,))) for p in terms)
-
-        def squares(c):
-            total = pf[use, c, 0] * pf[use, c, 0]
+            arrived(mc.at[pl.ds(0, NY - 1)], my_recv)
+        arrived(pf.at[use, pl.ds(0, NY - 1)], py_recv.at[use])
+        if use == 0:
+            norm = pf[use, 0] * pf[use, 0]
             for i in range(1, NY):
-                total = total + pf[use, c, i] * pf[use, c, i]
-            return total
-
-        def finish(gram):
-            return pack(gram[:, :RANK] + (gram[:, RANK : 2 * RANK] + gram[:, 2 * RANK :]))
-
-        terms = factors(k)
-        u_t = right(k, terms)
-        if use == 0:
-            norm = squares(k)
-            arrived(mc.at[1 - k], mk_recv)
-        else:
-            gram = square(terms)
-        arrived(pf.at[use, 1 - k], pk_recv.at[use])
-        terms = factors(1 - k)
-        u_t = u_t + right(1 - k, terms)
-        if use == 0:
-            norm = norm + squares(1 - k)
-            norm = jnp.sum(jnp.sum(norm, axis=1, keepdims=True), axis=0, keepdims=True)
-            return u_t, norm, lambda: finish(square(factors(0)) + square(factors(1)))
-        return u_t, finish(gram + square(terms))
+                norm = norm + pf[use, i] * pf[use, i]
+            nx[k] = (norm[:8] + norm[8:16]) + (norm[16:24] + norm[24:])
+            send(nx.at[k], nx.at[k], nx_send, nx_recv, partner)
+        terms = []
+        for i in range(0, NY, 4):
+            parts = []
+            for j in range(i, i + 4, 2):
+                one, two = pf[use, j], pf[use, j + 1]
+                upper = jnp.where(lane < RANK, one, pltpu.roll(two, RANK, 1))
+                lower = jnp.where(lane < RANK, pltpu.roll(one, RANK, 1), two)
+                parts.append(jnp.concatenate([upper, lower], axis=0))
+            terms.append(split(jnp.concatenate(parts, axis=1)))
+
+        def start_gram():
+            gram = sum(exact(p, p, ((1,), (1,))) for p in terms)
+            gx[use, k] = pack(gram[:, :RANK] + (gram[:, RANK : 2 * RANK] + gram[:, 2 * RANK :]))
+            send(gx.at[use, k], gx.at[use, k], gx_send, gx_recv.at[use], partner)
+
+        def start_right():
+            ux[use, k] = sum(exact(p, mc[4 * i : 4 * i + 4].reshape(4 * rows, cb)) for i, p in enumerate(terms))
+            send(ux.at[use, k], ux.at[use, k], ux_send, ux_recv.at[use], partner)
+
+        for start in (start_right, start_gram) if use == 0 else (start_gram, start_right):
+            start()
+
+        def gram():
+            arrived(gx.at[use, 1 - k], gx_recv.at[use])
+            return gx[use, 0] + gx[use, 1]
+
+        def right():
+            arrived(ux.at[use, 1 - k], ux_recv.at[use])
+            return ux[use, 0] + ux[use, 1]
+
+        return gram, right
 
     p, _ = sum_dp(
         lax.dot_general(q0[...], m, (((1,), (1,)), ((), ())), preferred_element_type=F32), 0
     )
-    u_t, norm, gram = over_rows(p, 0)
-    scale = lax.rsqrt(norm)
+    gram, right = over_rows(p, 0)
+    arrived(nx.at[1 - k], nx_recv)
+    scale = lax.rsqrt(jnp.sum(jnp.sum(nx[0] + nx[1], axis=0, keepdims=True), axis=1, keepdims=True))
+    u_t = right()
 
     p, inverse = sum_dp(
-        exact(split(u_t * scale), mc[k, y], ((1,), (1,))), 1, lambda: inverse_factor(gram() * scale * scale)
+        exact(split(u_t * scale), mc[y], ((1,), (1,))), 1, lambda: inverse_factor(gram() * scale * scale)
     )
     p_t = dot(inverse, unpack(p))
-    u_t, gram = over_rows(pack(p_t), 1)
-    inverse = inverse_factor(gram)
-    q_t = dot(inverse, u_t)
+    gram, right = over_rows(pack(p_t), 1)
+    inverse = inverse_factor(gram())
+    q_t = dot(inverse, right())
     qland[k, d] = jnp.where(k == 0, q_t[:, :half], q_t[:, half:]).astype(BF16)
 
-    for o in by_distance(NZ):
+    for o in by_distance(NZ)[::-1]:
         send(qland.at[k, d], qland.at[k, d], qz_send, qz_recv.at[o - 1], at_z(o))
     first, last = pl.ds(0, HALF), pl.ds(HALF, HALF)
 
@@ -304,7 +315,6 @@
 
     send(qland.at[k, d, last], qland.at[k, d, last], qv_send, qv_recv, at_x(opposite))
     to_x(d, 0)
-    send(qland.at[k, d], qland.at[k, d], qk_send, qk_recv, partner)
     basis[...] = dot(inverse, p_t).T.astype(BF16)
     facing = ((x + opposite) % NX) * NZ
     near = by_distance(NZ)[::-1]
@@ -312,11 +322,12 @@
         block = x * NZ + (z - o) % NZ
         arrived(qland.at[k, block], qz_recv.at[o - 1])
         to_x(block, o)
-        send(qland.at[k, block], qland.at[k, block], qk_send, qk_recv, partner)
         if i == 1:
             arrived(qland.at[k, facing + z, last], qv_recv)
             for zo in by_distance(NZ):
                 send(qland.at[k, facing + z, last], qland.at[k, facing + z, last], qv_send, qw_recv, at_z(zo))
+    column = qland.at[k, pl.ds(x * NZ, NZ)]
+    send(column, column, qk_send, qk_recv, partner)
     for o in [0] + near:
         arrived(qland.at[k, pl.ds(0, 2)], qx_recv.at[o])
         for j in range(2):
@@ -330,13 +341,14 @@
     left(xland, x_send)
     left(tland, t_send)
     left(tx, tx_send)
-    left(zland, z_send)
-    left(mc.at[k, pl.ds(0, NY - 1)], my_send)
-    left(mc.at[k], mk_send)
+    left(zsend, z_send)
+    left(mc.at[pl.ds(0, NY - 1)], my_send)
     left(px.at[:, pl.ds(0, NX - 1)], px_send)
     left(pz.at[:, pl.ds(0, NZ - 1)], pz_send)
-    left(pf.at[:, k, pl.ds(0, NY - 1)], py_send)
-    left(pf.at[:, k], pk_send)
+    left(pf.at[:, pl.ds(0, NY - 1)], py_send)
+    left(gx.at[:, k], gx_send)
+    left(ux.at[:, k], ux_send)
+    left(nx.at[k], nx_send)
     left(qland.at[k, pl.ds(0, NZ - 1)], qz_send)
     left(qland.at[k, pl.ds(0, 2 * NZ)], qx_send)
     left(qland.at[k, pl.ds(0, NZ), first], qu_send)
@@ -345,7 +357,7 @@
 
     @pl.when(is_source)
     def _():
-        left(mc.at[k], q0_send)
+        left(mc, q0_send)
 
     @pl.when(is_relay)
     def _():
@@ -395,19 +407,22 @@
         scratch_shapes=[
             pltpu.VMEM((rows, width), BF16),
             pltpu.VMEM((rows, width), BF16),
-            pltpu.VMEM((NZ, 3 * rows - TAIL, cb), BF16),
+            pltpu.VMEM((NZ // 2, 2, 3 * rows - TAIL, cb), BF16),
             pltpu.VMEM((NZ - 1, rows, cb), BF16),
-            pltpu.VMEM((NZ - 1, rows, cb), BF16),
+            pltpu.VMEM((NZ, rows, cb), BF16),
             pltpu.VMEM((NZ - 1, TAIL, cb), BF16),
             pltpu.VMEM((TAIL, cb), BF16),
             pltpu.VMEM((TAIL, cb), BF16),
-            pltpu.VMEM((2, NY, rows, cb), BF16),
+            pltpu.VMEM((NY, rows, cb), BF16),
             pltpu.VMEM((RANK, cb), BF16),
             pltpu.VMEM((2, NX) + small, F32),
             pltpu.VMEM((2, NZ) + small, F32),
-            pltpu.VMEM((2, 2, NY) + small, F32),
+            pltpu.VMEM((2, NY) + small, F32),
+            pltpu.VMEM((2, 2) + small, F32),
+            pltpu.VMEM((2, 2, RANK, cb), F32),
+            pltpu.VMEM((2, 8, 128), F32),
             dma((2,)), dma, dma, dma, dma, dma((NZ,)), dma, dma, dma, dma, dma, dma,
-            dma, dma, dma, dma, dma, dma((2,)), dma, dma((2,)), dma, dma((2,)), dma, dma((2,)),
+            dma, dma, dma, dma((2,)), dma, dma((2,)), dma, dma((2,)), dma, dma((2,)), dma, dma((2,)), dma, dma,
             dma, dma((NZ - 1,)), dma, dma((NZ,)), dma, dma, dma, dma, dma, dma, dma,
         ],
         compiler_params=pltpu.CompilerParams(collective_id=0, has_side_effects=True, vmem_limit_bytes=32 << 20),

time: 77.3 us -> 76.1 us (0.984)
  Pallas kernels: 76.5 us -> 75.4 us
    pallas_call x1, Pallas kernels: 74.9 us -> 73.8 us  [on_device(): pl.pallas_call(kernel, out_shape=(pltpu.VMEM((2, nd, RANK, cb // 2), BF16...]
where the time goes in v4:
time: 76.1 us; the launch traced here: 76 us
  Pallas kernels  75.4 us (99%)
    pallas_call x1, Pallas kernels, on_device(): pl.pallas_call(kernel, out_shape=(pltpu.VMEM((2, nd, RANK, cb // 2), BF16...  73.8 us
    pallas_call x1, Pallas kernels, on_device(): pl.pallas_call(decompress, out_shape=(jax.ShapeDtypeStruct((rows, width),...  1.58 us

profile of v4, /device:TPU:1, one launch (start us, length us, event | category | flops | bytes accessed | tf_op | source)
XLA Modules:
  0.0 76.0 jit_solution(3565231759224313749)
XLA Ops:
  0.6 73.8 %shard_map.50 = (bf16[2,32,64,128]{3,2,1,0:T(8,128)(2,1)S(1)}, bf16[32,64,256]{2,1,0:T(8,128)(2,1)S(1)}, bf16[64,64]{1,0:T(8,128)(2,1)S(1)}) custom-call(bf16[1,64,8192]{2,1,0:T(8,128)(2,1)} %g_ref.1, bf16[1,64,8192]{2,1,0:T(8,128)(2,1)} %e_ref.1, bf16[64,512]{1,0:T(8,128)(2,1)} %bitcast.1), custom_call_target="tpu_custom_call" | custom-call | flops 134217728 | bytes 4194304 | tf_op jit(solution)/shard_map/pallas_call | solution.py:398
  74.4 1.6 %shard_map.51 = (bf16[64,8192]{1,0:T(8,128)(2,1)}, bf16[1,64,8192]{2,1,0:T(8,128)(2,1)}) custom-call(bf16[2,32,64,128]{3,2,1,0:T(8,128)(2,1)S(1)} %get-tuple-element.5.q_ref, bf16[32,64,256]{2,1,0:T(8,128)(2,1)S(1)} %get-tuple-element.6.merged, bf16[64,64]{1,0:T(8,128)(2,1)S(1)} %get-tuple-element.7.basis), custom_call_target="tpu_custom_call" | custom-call | flops 67108864 | bytes 4194304 | tf_op jit(solution)/shard_map/pallas_call | solution.py:432

commit v5 on v4

--- a/solution.py
+++ b/solution.py
@@ -12,7 +12,7 @@
 NX, NY, NZ = 4, 8, 8
 RANK = 64
 HALF = RANK // 2
-TAIL = 32
+TAIL = 48
 GROUPS = 4
 
 
@@ -196,14 +196,14 @@
 
     for i in range(NZ // 2):
         if i == NZ // 2 - 1:
-            finish_tails()
-
             @pl.when(is_relay)
             def _():
                 arrived(q0, q0_recv)
                 send(q0, q0, q0_send, q0_recv, partner)
 
         arrived(xland.at[i], x_recv.at[i])
+        if i == NZ // 2 - 1:
+            finish_tails()
         for b in range(2) if i < NZ // 2 - 1 else (1 - z % 2,):
             at = 2 * i if i == NZ // 2 - 1 else 2 * i + b
             zsend[at] = block_sum(i, b).astype(BF16)
@@ -242,7 +242,7 @@
 
     lane = lax.broadcasted_iota(jnp.int32, (HALF, 2 * RANK), 1)
 
-    def over_rows(packed, use):
+    def over_rows(packed, use, factor=None):
         pf[use, y] = packed
         for o in by_distance(NY):
             send(pf.at[use, y], pf.at[use, y], py_send, py_recv.at[use], at_y(o))
@@ -263,7 +263,8 @@
                 upper = jnp.where(lane < RANK, one, pltpu.roll(two, RANK, 1))
                 lower = jnp.where(lane < RANK, pltpu.roll(one, RANK, 1), two)
                 parts.append(jnp.concatenate([upper, lower], axis=0))
-            terms.append(split(jnp.concatenate(parts, axis=1)))
+            p = jnp.concatenate(parts, axis=1)
+            terms.append(split(p if factor is None else dot(factor, p)))
 
         def start_gram():
             gram = sum(exact(p, p, ((1,), (1,))) for p in terms)
@@ -298,8 +299,8 @@
     p, inverse = sum_dp(
         exact(split(u_t * scale), mc[y], ((1,), (1,))), 1, lambda: inverse_factor(gram() * scale * scale)
     )
+    gram, right = over_rows(p, 1, inverse)
     p_t = dot(inverse, unpack(p))
-    gram, right = over_rows(pack(p_t), 1)
     inverse = inverse_factor(gram())
     q_t = dot(inverse, right())
     qland[k, d] = jnp.where(k == 0, q_t[:, :half], q_t[:, half:]).astype(BF16)

time: 76.1 us -> 74.3 us (0.976)
  Pallas kernels: 75.4 us -> 73.6 us
    pallas_call x1, Pallas kernels: 73.8 us -> 72 us  [on_device(): pl.pallas_call(kernel, out_shape=(pltpu.VMEM((2, nd, RANK, cb // 2), BF16...]
where the time goes in v5:
time: 74.3 us; the launch traced here: 74.2 us
  Pallas kernels  73.6 us (99%)
    pallas_call x1, Pallas kernels, on_device(): pl.pallas_call(kernel, out_shape=(pltpu.VMEM((2, nd, RANK, cb // 2), BF16...  72 us
    pallas_call x1, Pallas kernels, on_device(): pl.pallas_call(decompress, out_shape=(jax.ShapeDtypeStruct((rows, width),...  1.58 us

profile of v5, /device:TPU:1, one launch (start us, length us, event | category | flops | bytes accessed | tf_op | source)
XLA Modules:
  0.0 74.2 jit_solution(11007243530886330947)
XLA Ops:
  0.6 72.0 %shard_map.50 = (bf16[2,32,64,128]{3,2,1,0:T(8,128)(2,1)S(1)}, bf16[32,64,256]{2,1,0:T(8,128)(2,1)S(1)}, bf16[64,64]{1,0:T(8,128)(2,1)S(1)}) custom-call(bf16[1,64,8192]{2,1,0:T(8,128)(2,1)} %g_ref.1, bf16[1,64,8192]{2,1,0:T(8,128)(2,1)} %e_ref.1, bf16[64,512]{1,0:T(8,128)(2,1)} %bitcast.1), custom_call_target="tpu_custom_call" | custom-call | flops 134217728 | bytes 4194304 | tf_op jit(solution)/shard_map/pallas_call | solution.py:399
  72.6 1.6 %shard_map.51 = (bf16[64,8192]{1,0:T(8,128)(2,1)}, bf16[1,64,8192]{2,1,0:T(8,128)(2,1)}) custom-call(bf16[2,32,64,128]{3,2,1,0:T(8,128)(2,1)S(1)} %get-tuple-element.5.q_ref, bf16[32,64,256]{2,1,0:T(8,128)(2,1)S(1)} %get-tuple-element.6.merged, bf16[64,64]{1,0:T(8,128)(2,1)S(1)} %get-tuple-element.7.basis), custom_call_target="tpu_custom_call" | custom-call | flops 67108864 | bytes 4194304 | tf_op jit(solution)/shard_map/pallas_call | solution.py:433

commit v6 on v5

--- a/solution.py
+++ b/solution.py
@@ -307,7 +307,7 @@
 
     for o in by_distance(NZ)[::-1]:
         send(qland.at[k, d], qland.at[k, d], qz_send, qz_recv.at[o - 1], at_z(o))
-    first, last = pl.ds(0, HALF), pl.ds(HALF, HALF)
+    first, last = pl.ds(0, RANK // 4), pl.ds(RANK // 4, 3 * RANK // 4)
 
     def to_x(block, at):
         send(qland.at[k, block, first], qland.at[k, block, first], qu_send, qu_recv, at_x(opposite))

time: 74.3 us -> 74.2 us (level)
  no operation moved by 1% of the time
where the time goes in v6:
time: 74.2 us; the launch traced here: 74 us
  Pallas kernels  73.4 us (99%)
    pallas_call x1, Pallas kernels, on_device(): pl.pallas_call(kernel, out_shape=(pltpu.VMEM((2, nd, RANK, cb // 2), BF16...  71.8 us
    pallas_call x1, Pallas kernels, on_device(): pl.pallas_call(decompress, out_shape=(jax.ShapeDtypeStruct((rows, width),...  1.58 us

profile of v6, /device:TPU:1, one launch (start us, length us, event | category | flops | bytes accessed | tf_op | source)
XLA Modules:
  0.0 74.0 jit_solution(9719066849007251361)
XLA Ops:
  0.6 71.8 %shard_map.50 = (bf16[2,32,64,128]{3,2,1,0:T(8,128)(2,1)S(1)}, bf16[32,64,256]{2,1,0:T(8,128)(2,1)S(1)}, bf16[64,64]{1,0:T(8,128)(2,1)S(1)}) custom-call(bf16[1,64,8192]{2,1,0:T(8,128)(2,1)} %g_ref.1, bf16[1,64,8192]{2,1,0:T(8,128)(2,1)} %e_ref.1, bf16[64,512]{1,0:T(8,128)(2,1)} %bitcast.1), custom_call_target="tpu_custom_call" | custom-call | flops 134217728 | bytes 4194304 | tf_op jit(solution)/shard_map/pallas_call | solution.py:399
  72.5 1.6 %shard_map.51 = (bf16[64,8192]{1,0:T(8,128)(2,1)}, bf16[1,64,8192]{2,1,0:T(8,128)(2,1)}) custom-call(bf16[2,32,64,128]{3,2,1,0:T(8,128)(2,1)S(1)} %get-tuple-element.5.q_ref, bf16[32,64,256]{2,1,0:T(8,128)(2,1)S(1)} %get-tuple-element.6.merged, bf16[64,64]{1,0:T(8,128)(2,1)S(1)} %get-tuple-element.7.basis), custom_call_target="tpu_custom_call" | custom-call | flops 67108864 | bytes 4194304 | tf_op jit(solution)/shard_map/pallas_call | solution.py:433
